TPU v7x, 32 devices: a whole 2x2x4 slice. The times are simulated.
32 devices in a mesh: rows: 4 (over y, x), half: 2 (over core), obs: 4 (over z).
Axes of the slice: x: 2, y: 2, z: 4, core: 2. Of those that a mesh axis runs over, the one named last changes fastest.
Arguments:
- ens_state: bfloat16 [2, 8192, 256], P('half', ('rows', 'obs')), may hold values from -6 to 6
- state_pos: bfloat16 [8192], P(('rows', 'obs')), may hold values from 0 to 1
- obs_ens: bfloat16 [2, 2, 8192, 256], P(None, 'half', ('rows', 'obs')), may hold values from -6 to 6
- obs_pos: bfloat16 [2, 8192], P(None, ('rows', 'obs')), may hold values from 0 to 1
- innov_weight: bfloat16 [2, 2, 8192, 256], P(None, 'half', ('rows', 'obs')), may hold values from -0.875 to 0.875
- block_rows: int32 [2, 64, 16], replicated, may hold values from 0 to 63, as said below
Outputs:
- increment: float32 [2, 8192, 256], P('half', ('rows', 'obs'))
Inputs may be any that keep to these rules, and one draw needn't show every extreme that they name: `block_rows`: each row lists 16 different state blocks. Counting state blocks in aligned ranges of 16, an observation block names at most 8 blocks of one range, and in every aligned group of 16 observation blocks some range is named exactly 8 times by each block of the group.
All inputs are finite; a program needn't handle non-finite values.
Results may differ from a plain program's by a relative error of at most 0.0029.
Values may be sent and summed in bfloat16 or wider, within the bound.
A program may use at most 64 MiB of HBM per device.

v0:
```python
import jax
import jax.numpy as jnp
from jax import lax
from jax.sharding import PartitionSpec as P

ROW_BLOCKS = 16
OBS_BLOCKS = 16
BATCHES = 2


def partner(value, axis, bit):
    mask = 2**bit
    pairs = [(source, source ^ mask) for source in range(lax.axis_size(axis))]
    return lax.ppermute(value, axis, pairs)


def slot_tables(picked, first_block, row_blocks):
    blocks_iota = jnp.arange(row_blocks, dtype=jnp.int32)
    relative = picked - first_block
    present = jnp.sum(
        (relative[:, :, None] == blocks_iota[None, None, :]).astype(jnp.int32), axis=1
    )
    ranking = jnp.cumsum(present, axis=1) - 1
    slot_iota = jnp.arange(row_blocks // 2, dtype=jnp.int32)
    chosen = present[:, :, None] * (ranking[:, :, None] == slot_iota[None, None, :]).astype(
        jnp.int32
    )
    slot_block = jnp.sum(chosen * blocks_iota[None, :, None], axis=1)
    slot_live = jnp.sum(chosen, axis=1)
    return (slot_block, slot_live)


def batch_increment(state_rows, row_places, obs_rows, obs_places, weights, picked, first_block):
    row_blocks = ROW_BLOCKS
    edge_size = obs_rows.shape[0] // picked.shape[0]
    member_count = state_rows.shape[1]
    state_tiles = state_rows.reshape(row_blocks, edge_size, member_count)
    place_tiles = row_places.astype(jnp.float32).reshape(row_blocks, edge_size)
    slot_block, slot_live = slot_tables(picked, first_block, row_blocks)

    def visit(running, entries):
        obs_tile, obs_place, weight_tile, blocks_here, live_here = entries
        gathered = state_tiles[blocks_here].reshape(-1, member_count)
        positions = place_tiles[blocks_here].reshape(-1)
        products = lax.dot_general(
            gathered, obs_tile, (((1,), (1,)), ((), ())), preferred_element_type=jnp.float32
        )
        distance = positions[:, None] - obs_place[None, :]
        damping = jnp.exp(-4.0 * distance * distance)
        live_rows = jnp.repeat(live_here.astype(jnp.float32), edge_size)
        scaled = (products * damping / (member_count - 1) * live_rows[:, None]).astype(jnp.bfloat16)
        additions = jnp.dot(scaled, weight_tile, preferred_element_type=jnp.float32)
        running = running.at[blocks_here].add(additions.reshape(-1, edge_size, member_count))
        return (running, None)

    initial = jnp.zeros((row_blocks, edge_size, member_count), jnp.float32)
    entries = (
        obs_rows.reshape(-1, edge_size, member_count),
        obs_places.astype(jnp.float32).reshape(-1, edge_size),
        weights.reshape(-1, edge_size, member_count),
        slot_block,
        slot_live,
    )
    running, _ = lax.scan(visit, initial, entries)
    return running.reshape(row_blocks * edge_size, member_count)


def local(ens_state, state_pos, obs_ens, obs_pos, innov_weight, block_rows):
    state_own, obs_own = partner((ens_state, obs_ens), "half", 0)
    place_column = obs_pos[:, None, :, None]
    obs_full, weight_full, place_full_obs = (
        lax.all_gather(obs_own, "rows", axis=2, tiled=True),
        lax.all_gather(innov_weight, "rows", axis=2, tiled=True),
        lax.all_gather(place_column, "rows", axis=2, tiled=True),
    )
    state_full, place_full = (
        lax.all_gather(state_own[0], "obs", axis=0, tiled=True),
        lax.all_gather(state_pos, "obs", axis=0, tiled=True),
    )
    first_block = lax.axis_index("rows") * ROW_BLOCKS
    obs_count = lax.axis_size("obs")
    row_count = lax.axis_size("rows")
    span_blocks = OBS_BLOCKS // row_count
    block_ids = (
        (jnp.arange(row_count, dtype=jnp.int32)[:, None] * obs_count + lax.axis_index("obs"))
        * span_blocks
        + jnp.arange(span_blocks, dtype=jnp.int32)[None, :]
    ).reshape(-1)
    shares = None
    summed = None
    for batch_index in range(BATCHES):
        picked_here = block_rows[batch_index][block_ids]
        partial_value = batch_increment(
            state_full,
            place_full,
            obs_full[batch_index, 0],
            place_full_obs[batch_index, 0, :, 0],
            weight_full[batch_index, 0],
            picked_here,
            first_block,
        )
        summed = partial_value if summed is None else summed + partial_value
    shares = lax.psum_scatter(summed, "obs", scatter_dimension=0, tiled=True)
    return shares[None]


def solution(mesh):
    in_specs = (
        P("half", ("rows", "obs"), None),
        P(("rows", "obs")),
        P(None, "half", ("rows", "obs"), None),
        P(None, ("rows", "obs")),
        P(None, "half", ("rows", "obs"), None),
        P(),
    )
    out_specs = P("half", ("rows", "obs"), None)
    return jax.shard_map(local, mesh=mesh, in_specs=in_specs, out_specs=out_specs, check_vma=False)
```

profile of v0, /device:TPU:0, one launch (start us, length us, event | category | flops | bytes accessed | tf_op | source)
XLA Modules:
  0.0 366.9 jit_solution(16243886209917230550)
XLA Ops:
  14.8 13.2 %all-gather.2 = bf16[4,1,512]{2,1,0:T(2,128)(2,1)S(1)} all-gather(bf16[1,1,512]{2,1,0:T(2,128)(2,1)S(1)} %reshape.247), channel_id=1, replica_groups=mesh['rows'=4,'half'=2,'obs'=4] {'obs'}, dimensions={0}, use_global_device_ids=true | all-gather | bytes 5120 | tf_op jit(solution)/shard_map/all_gather | solution.py:78
  28.2 8.2 %all-gather.1 = bf16[2,2048]{1,0:T(2,128)(2,1)S(1)} all-gather(bf16[2,512]{1,0:T(2,128)(2,1)} %param.13), channel_id=3, replica_groups=mesh['rows'=4,'half'=2,'obs'=4] {'rows'}, dimensions={1}, use_global_device_ids=true | all-gather | bytes 10240 | tf_op jit(solution)/shard_map/all_gather | solution.py:74
  37.8 9.4 %all-gather.9.cloned.1.call-done = bf16[2,1,2048,256]{3,2,1,0:T(8,128)(2,1)} async-done(((bf16[2,1,512,256]{3,2,1,0:T(8,128)(2,1)}), bf16[2,1,2048,256]{3,2,1,0:T(8,128)(2,1)}) %all-gather.9.cloned.1.call-update) | async-done | bytes 2097168 | tf_op jit(solution)/shard_map/all_gather | solution.py:73
  47.3 3.0 fusion.35
  50.3 34.2 %all-gather.7.cloned.1.call-done = bf16[2,1,2048,256]{3,2,1,0:T(8,128)(2,1)} async-done(((bf16[2,1,512,256]{3,2,1,0:T(8,128)(2,1)}), bf16[2,1,2048,256]{3,2,1,0:T(8,128)(2,1)}) %all-gather.7.cloned.1.call-update) | async-done | bytes 2097168 | tf_op jit(solution)/shard_map/all_gather | solution.py:72
  84.4 3.0 fusion.36
  87.4 26.6 %all-gather.11.cloned.1.call-done = bf16[1,2048,256]{2,1,0:T(8,128)(2,1)} async-done(((bf16[1,512,256]{2,1,0:T(8,128)(2,1)}), bf16[1,2048,256]{2,1,0:T(8,128)(2,1)}) %all-gather.11.cloned.1.call-update) | async-done | bytes 1048592 | tf_op jit(solution)/shard_map/all_gather | solution.py:77
  114.2 99.1 %while.21 = (s32[]{:T(128)}, f32[16,128,256]{2,1,0:T(8,128)S(1)}, s32[16,8]{1,0:T(8,128)S(1)}, bf16[16,128,256]{2,1,0:T(8,128)(2,1)}, bf16[16,128,256]{2,1,0:T(8...) while((s32[]{:T(128)}, f32[16,128,256]{2,1,0:T(8,128)S(1)}, ...), condition=%wide.region_13.14_spmd, body=%wide.region_11.13_spmd.sunk | while | flops 135267360 | bytes 6450065 | solution.py:64
  114.2 1.8 gather_fusion.2
  120.4 1.8 gather_fusion.2
  126.6 1.8 gather_fusion.2
  132.8 1.8 gather_fusion.2
  139.0 1.8 gather_fusion.2
  145.2 1.8 gather_fusion.2
  151.4 1.8 gather_fusion.2
  163.8 1.8 gather_fusion.2
  170.0 1.8 gather_fusion.2
  176.2 1.8 gather_fusion.2
  194.7 1.8 gather_fusion.2
  200.9 1.8 gather_fusion.2
  214.9 98.9 %while.20 = (s32[]{:T(128)}, f32[16,128,256]{2,1,0:T(8,128)S(1)}, s32[16,8]{1,0:T(8,128)S(1)}, bf16[16,128,256]{2,1,0:T(8,128)(2,1)}, bf16[16,128,256]{2,1,0:T(8...) while((s32[]{:T(128)}, f32[16,128,256]{2,1,0:T(8,128)S(1)}, ...), condition=%wide.region_6.7_spmd, body=%wide.region_4.6_spmd.sunk | while | flops 135267360 | bytes 6450065 | solution.py:64
  214.9 1.8 gather_fusion
  221.1 1.8 gather_fusion
  227.3 1.8 gather_fusion
  233.5 1.8 gather_fusion
  239.7 1.8 gather_fusion
  245.9 1.8 gather_fusion
  252.1 1.8 gather_fusion
  258.2 1.8 gather_fusion
  270.6 1.8 gather_fusion
  313.8 3.3 add.105
  317.1 43.3 %reduce-scatter.2.cloned.1.call-done = f32[512,256]{1,0:T(8,128)} async-done(((f32[2048,256]{1,0:T(8,128)}), f32[512,256]{1,0:T(8,128)}) %reduce-scatter.2.cloned.1.call-update) | async-done | bytes 524304 | tf_op jit(solution)/shard_map/reduce_scatter | solution.py:103
  (341 shorter events, 169.6 us)
Async XLA Ops:
  6.5 40.7 %all-gather.9.cloned.1.call-start = ((), (), s32[]{:S(2)}) async-start(), calls=%async_computation.2 | async-start | bytes 2621440 | tf_op jit(solution)/shard_map/all_gather | solution.py:73
  7.3 77.2 %all-gather.7.cloned.1.call-start = ((), (), s32[]{:S(2)}) async-start(), calls=%async_computation.1 | async-start | bytes 2621440 | tf_op jit(solution)/shard_map/all_gather | solution.py:72
  7.3 2.3 collective-permute-start.1
  9.6 0.8 copy-start.1
  10.4 103.6 %all-gather.11.cloned.1.call-start = ((), (), s32[]{:S(2)}) async-start(), calls=%async_computation.4 | async-start | bytes 1310720 | tf_op jit(solution)/shard_map/all_gather | solution.py:77
  10.4 26.0 %collective-permute-start = (bf16[1,512,256]{2,1,0:T(8,128)(2,1)}, bf16[1,512,256]{2,1,0:T(8,128)(2,1)S(1)}, u32[]{:S(2)}, u32[]{:S(2)}) collective-permute-start(bf16[1,512,256]{2,1,0:T(8,128)(2,1)} %param.10), channel_id=1, source_target_pairs={{0,4},{4,0},{1,5},{5,1},{2,6},{6,2},{3,7},{7,3},{8,12},{12,8},{9,1... | collective-permute-start | bytes 786440 | tf_op jit(solution)/shard_map/ppermute | solution.py:14
  36.4 0.7 copy-start.2
  37.2 323.3 %reduce-scatter.2.cloned.1.call-start = ((), (), s32[]{:S(2)}) async-start(), calls=%async_computation.3 | async-start | bytes 2621440 | tf_op jit(solution)/shard_map/reduce_scatter | solution.py:103
  213.3 1.4 copy-start
Sparse Core Ops, SparseCore 0:
  9.2 38.0 all-gather.8
  49.1 35.2 all-gather.6
  86.0 27.9 all-gather.10
  317.3 43.1 reduce-scatter.1
where the time goes:
time: 372 us; the launch traced here: 367 us
  waiting for transfers between devices  116 us (31%)
  local copies, waits for them, and re-layouts  89.9 us (24%)
  matrix products  74.4 us (20%)
  other arithmetic  48.8 us (13%)
  blocking collectives  21.4 us (6%)
  between operations  13.3 us (4%)
    gather x32, local copies, waits for them, and re-layouts, visit(): gathered = state_tiles[blocks_here].reshape(-1, member_count)  57.8 us
    reduce_scatter x1, waiting for transfers between devices, local(): shares = lax.psum_scatter(summed, 'obs', scatter_dimension=0, tiled=True)  43.3 us
    scatter-add x32, other arithmetic, visit(): running.at[blocks_here].add(additions.reshape(-1, edge_size, member_count))  42.6 us
    dot_general x32, matrix products, visit(): lax.dot_general(gathered, obs_tile, (((1,), (1,)), ((), ())), preferred_e...  38.7 us
    dot_general x32, matrix products, visit(): additions = jnp.dot(scaled, weight_tile, preferred_element_type=jnp.float32)  35.7 us
    all_gather x1, waiting for transfers between devices, local(): lax.all_gather(obs_own, 'rows', axis=2, tiled=True)  34.2 us
    all_gather x1, waiting for transfers between devices, local(): lax.all_gather(state_own[0], 'obs', axis=0, tiled=True)  26.6 us
    gather x32, local copies, waits for them, and re-layouts, visit(): positions = place_tiles[blocks_here].reshape(-1)  17.8 us
  transfers between devices with their start and end apart: 6, of which 5 were waited for; matrix products, arithmetic and copies ran while one was open for 3% of the time, Pallas kernels for 0%

commit v1 on v0

v1 whole, which is shorter than its diff:
```python
import functools
import math

import jax
import jax.numpy as jnp
from jax import lax
from jax.experimental import pallas as pl
from jax.experimental.pallas import tpu as pltpu
from jax.sharding import PartitionSpec as P

LANES = 128
UNIT = 256
STRETCH = 2.0 * math.sqrt(math.log2(math.e))
MASKED = -1e30


def kernel(sizes, state_ref, place_ref, obs_ref, obs_place_ref, weight_ref, named_ref, out_ref,
           states, columns, obs, weights, places, place_send, obs_places, obs_place_send, masks, total, shares, arrived,
           state_s, state_r, place_s, place_r, obs_s, obs_r, weight_s, weight_r, op_s, op_r, share_s, share_r, own_sem):
    n_rows, n_obs, own_rows, obs_rows, blocks, batches = sizes
    edge = obs_rows // blocks
    members = state_ref.shape[-1]
    span = n_obs * own_rows
    span_blocks = span // edge
    r, h, o = lax.axis_index("rows"), lax.axis_index("half"), lax.axis_index("obs")
    flip = 1 - h
    forward = n_rows == 4
    direct = (1, 2) if forward else tuple(range(1, n_rows))

    def at(row, half, column):
        return {"rows": row, "half": half, "obs": column}

    def remote(src, dst, send, recv, device):
        return pltpu.make_async_remote_copy(src_ref=src, dst_ref=dst, send_sem=send, recv_sem=recv,
                                            device_id=device, device_id_type=pl.DeviceIdType.MESH)

    def other(k):
        return lax.rem(o + k, n_obs)

    place_send[...] = place_ref[...].astype(jnp.float32) * STRETCH
    obs_place_send[...] = obs_place_ref[...].astype(jnp.float32) * STRETCH
    places[o] = place_send[...]
    obs_places[0] = obs_place_send[...]

    barrier = pltpu.get_barrier_semaphore()

    def greet(device):
        pl.semaphore_signal(barrier, inc=1, device_id=device, device_id_type=pl.DeviceIdType.MESH)

    greet(at(r, flip, o))
    for k in range(1, n_obs):
        greet(at(r, h, other(k)))
        greet(at(r, flip, other(k)))
    for delta in range(1, n_rows):
        greet(at(r ^ delta, h, o))
        greet(at(r ^ delta, flip, o))
    pl.semaphore_wait(barrier, 1 + 2 * (n_obs - 1) + 2 * (n_rows - 1))

    def state_slot(source):
        return states.at[pl.ds(pl.multiple_of(source * own_rows, own_rows), own_rows)]

    def state_copy(k):
        return remote(state_ref.at[0], state_slot(o), state_s.at[k], state_r.at[k], at(r, flip, other(k)))

    def state_arrival(k):
        source = lax.rem(o - k + n_obs, n_obs)
        return remote(state_ref.at[0], state_slot(source), state_s.at[k], state_r.at[k], at(r, flip, other(k)))

    def place_copy(k):
        return remote(place_send, places.at[o], place_s.at[k], place_r.at[k], at(r, h, other(k)))

    def place_arrival(k):
        source = lax.rem(o - k + n_obs, n_obs)
        return remote(place_send, places.at[source], place_s.at[k], place_r.at[k], at(r, h, other(k)))

    def obs_copy(delta, t):
        return remote(obs_ref.at[t, 0], obs.at[delta, t], obs_s.at[delta, t], obs_r.at[delta, t], at(r ^ delta, flip, o))

    def weight_copy(delta, t):
        return remote(weight_ref.at[t, 0], weights.at[delta, t], weight_s.at[delta, t], weight_r.at[delta, t],
                      at(r ^ delta, h, o))

    def obs_place_copy(delta):
        return remote(obs_place_send, obs_places.at[delta], op_s.at[delta], op_r.at[delta], at(r ^ delta, h, o))

    def obs_forward(t):
        came, goes = (1, 2) if t % 2 == 0 else (2, 1)
        return remote(obs.at[came, t], obs.at[3, t], obs_s.at[3, t], obs_r.at[3, t], at(r ^ goes, h, o))

    def weight_forward(t):
        came, goes = (1, 2) if t % 2 == 0 else (2, 1)
        return remote(weights.at[came, t], weights.at[3, t], weight_s.at[3, t], weight_r.at[3, t], at(r ^ goes, h, o))

    own_weights = [pltpu.make_async_copy(weight_ref.at[t, 0], weights.at[0, t], own_sem.at[t]) for t in range(batches)]

    for k in range(1, n_obs):
        place_copy(k).start()
    for delta in range(1, n_rows):
        obs_place_copy(delta).start()
    order = {1: [t for t in range(batches) if t % 2 == 0] + [t for t in range(batches) if t % 2],
             2: [t for t in range(batches) if t % 2] + [t for t in range(batches) if t % 2 == 0]}
    for step in range(batches):
        for delta in direct:
            t = order[delta][step] if delta in order else step
            obs_copy(delta, t).start()
            weight_copy(delta, t).start()
        if step == 0:
            state_copy(0).start()
            for t in range(batches):
                obs_copy(0, t).start()
                own_weights[t].start()
            for k in range(1, n_obs):
                state_copy(k).start()

    kept = -math.log2(members - 1)
    first = r * span_blocks
    ids = lax.broadcasted_iota(jnp.int32, (span_blocks, 1), 0) + first
    for delta in range(n_rows):
        base = ((r ^ delta) * n_obs + o) * blocks
        for t in range(batches):
            def fill(b, carry, base=base, delta=delta, t=t):
                named = named_ref[t, pl.ds(base + b, 1), :]
                listed = jnp.max(jnp.where(named == ids, 1.0, 0.0), axis=1, keepdims=True)
                masks[delta, t, b] = jnp.broadcast_to(jnp.where(listed > 0.5, kept, MASKED), (span_blocks, edge))
                return carry
            lax.fori_loop(0, blocks, fill, 0)

    total[...] = jnp.zeros_like(total)

    for k in range(1, n_obs):
        place_arrival(k).wait_recv()
    for delta in range(1, n_rows):
        obs_place_copy(delta).wait_recv()

    def stand(source, carry):
        for piece in range(-(-own_rows // LANES)):
            count = min(LANES, own_rows - piece * LANES)
            row = places[source, :, piece * LANES:(piece + 1) * LANES]
            column = jnp.broadcast_to(row, (LANES, LANES)).T
            start = pl.multiple_of(source * own_rows, own_rows) + piece * LANES
            columns[pl.ds(start, count), :] = column[:count]
        return carry
    lax.fori_loop(0, n_obs, stand, 0)

    def unit(delta, t, index):
        start = pl.multiple_of(index * UNIT, UNIT)
        products = lax.dot_general(states[pl.ds(start, UNIT), :], obs[delta, t], (((1,), (1,)), ((), ())),
                                   preferred_element_type=jnp.float32)
        parts = []
        for b in range(blocks):
            y = obs_places[delta, t, :, b * edge:(b + 1) * edge]
            rows = []
            for q in range(UNIT // edge):
                x = columns[pl.ds(start + q * edge, edge), :]
                m = masks[delta, t, b, pl.ds(index * (UNIT // edge) + q, 1), :]
                d = x - y
                damping = jnp.exp2(m - d * d)
                rows.append((products[q * edge:(q + 1) * edge, b * edge:(b + 1) * edge] * damping).astype(jnp.bfloat16))
            parts.append(jnp.concatenate(rows, axis=0))
        tiles = jnp.concatenate(parts, axis=1)
        total[pl.ds(start, UNIT), :] += jnp.dot(tiles, weights[delta, t], preferred_element_type=jnp.float32)

    def pieces_in(delta, t):
        obs_copy(delta, t).wait_recv()
        if delta:
            weight_copy(delta, t).wait_recv()
        else:
            own_weights[t].wait()

    if forward:
        for t in range(batches):
            came = 1 if t % 2 == 0 else 2
            pieces_in(came, t)
            obs_forward(t).start()
            weight_forward(t).start()
        done = {(1 if t % 2 == 0 else 2, t) for t in range(batches)}
    else:
        done = set()

    for k in range(n_obs):
        state_arrival(k).wait_recv()

    chunks = [(0, t) for t in range(batches)] + sorted(done)
    chunks += [(d, t) for d in range(1, n_rows) for t in range(batches) if (d, t) not in done]
    last = chunks[-batches:]
    for chunk in chunks[:-batches]:
        if chunk not in done:
            pieces_in(*chunk)

        def sweep(index, carry, chunk=chunk):
            unit(*chunk, index)
            return carry
        lax.fori_loop(0, span // UNIT, sweep, 0)

    for chunk in last:
        if chunk not in done:
            pieces_in(*chunk)

    group = max(UNIT, own_rows)
    groups = span // group
    own_group = o // (group // own_rows)

    def share_copy(d):
        return remote(shares.at[pl.ds(pl.multiple_of(d * own_rows, own_rows), own_rows)], arrived.at[o],
                      share_s.at[d], share_r.at[o], at(r, h, d))

    def finish(g, carry):
        which = lax.rem(own_group + 1 + g, groups)
        for u in range(group // UNIT):
            for chunk in last:
                unit(*chunk, which * (group // UNIT) + u)
        start = pl.multiple_of(which * group, group)
        shares[pl.ds(start, group), :] = total[pl.ds(start, group), :].astype(jnp.bfloat16)
        for j in range(group // own_rows):
            d = which * (group // own_rows) + j

            @pl.when(d != o)
            def _():
                share_copy(d).start()
        return carry
    lax.fori_loop(0, groups, finish, 0)

    mine = pl.multiple_of(o * own_rows, own_rows)

    out_ref[0] = total[pl.ds(mine, own_rows), :]

    def collect(k, carry):
        source = other(k)
        remote(shares.at[pl.ds(mine, own_rows)], arrived.at[source], share_s.at[source], share_r.at[source],
               at(r, h, source)).wait_recv()
        out_ref[0] += arrived[source].astype(jnp.float32)
        return carry
    lax.fori_loop(1, n_obs, collect, 0)

    def left(k, carry):
        share_copy(other(k)).wait_send()
        return carry
    lax.fori_loop(1, n_obs, left, 0)
    for k in range(n_obs):
        state_copy(k).wait_send()
        if k:
            place_copy(k).wait_send()
    for delta in range(n_rows):
        if delta:
            obs_place_copy(delta).wait_send()
        for t in range(batches):
            if delta == 0 or delta in direct:
                obs_copy(delta, t).wait_send()
                if delta:
                    weight_copy(delta, t).wait_send()
    if forward:
        for t in range(batches):
            obs_forward(t).wait_send()
            weight_forward(t).wait_send()


def local(mesh_shape, ens_state, state_pos, obs_ens, obs_pos, innov_weight, block_rows):
    n_rows, n_obs = mesh_shape["rows"], mesh_shape["obs"]
    own_rows, members = ens_state.shape[1:]
    batches, _, obs_rows, _ = obs_ens.shape
    blocks = block_rows.shape[1] // (n_rows * n_obs)
    edge = obs_rows // blocks
    span = n_obs * own_rows
    sizes = (n_rows, n_obs, own_rows, obs_rows, blocks, batches)
    place_row = state_pos[None, :]
    width = -(-own_rows // LANES) * LANES
    if width != own_rows:
        place_row = jnp.pad(place_row, ((0, 0), (0, width - own_rows)))
    dma = pltpu.SemaphoreType.DMA
    f32, bf16 = jnp.float32, jnp.bfloat16
    whole = pl.BlockSpec(memory_space=pltpu.VMEM)
    hbm = pl.BlockSpec(memory_space=pl.ANY)
    return pl.pallas_call(
        functools.partial(kernel, sizes),
        out_shape=jax.ShapeDtypeStruct(ens_state.shape, f32),
        in_specs=[hbm, whole, hbm, whole, hbm, whole],
        out_specs=whole,
        scratch_shapes=[
            pltpu.VMEM((span, members), bf16),
            pltpu.VMEM((span, LANES), f32),
            pltpu.VMEM((n_rows, batches, obs_rows, members), bf16),
            pltpu.VMEM((n_rows, batches, obs_rows, members), bf16),
            pltpu.VMEM((n_obs, 1, width), f32),
            pltpu.VMEM((1, width), f32),
            pltpu.VMEM((n_rows, batches, 1, obs_rows), f32),
            pltpu.VMEM((batches, 1, obs_rows), f32),
            pltpu.VMEM((n_rows, batches, blocks, span // edge, edge), f32),
            pltpu.VMEM((span, members), f32),
            pltpu.VMEM((span, members), bf16),
            pltpu.VMEM((n_obs, own_rows, members), bf16),
            dma((n_obs,)), dma((n_obs,)), dma((n_obs,)), dma((n_obs,)),
            dma((n_rows, batches)), dma((n_rows, batches)), dma((n_rows, batches)), dma((n_rows, batches)),
            dma((n_rows,)), dma((n_rows,)), dma((n_obs,)), dma((n_obs,)), dma((batches,)),
        ],
        compiler_params=pltpu.CompilerParams(collective_id=0, has_side_effects=True, vmem_limit_bytes=48 * 2**20),
        cost_estimate=pl.CostEstimate(flops=4 * span * members * n_rows * batches * obs_rows,
                                      bytes_accessed=4 * 2**20,
                                      transcendentals=span * n_rows * batches * obs_rows),
    )(ens_state, place_row, obs_ens, obs_pos[:, None, :], innov_weight, block_rows)


def solution(mesh):
    in_specs = (
        P("half", ("rows", "obs"), None),
        P(("rows", "obs")),
        P(None, "half", ("rows", "obs"), None),
        P(None, ("rows", "obs")),
        P(None, "half", ("rows", "obs"), None),
        P(),
    )
    out_specs = P("half", ("rows", "obs"), None)
    return jax.shard_map(functools.partial(local, dict(mesh.shape)), mesh=mesh, in_specs=in_specs,
                         out_specs=out_specs, check_vma=False)
```

time: 372 us -> 80.1 us (0.22)
  the two profiles are of different devices: /device:TPU:0 before, /device:TPU:25 now
where the time goes in v1:
time: 80.1 us; the launch traced here: 79.8 us
  Pallas kernels  74.4 us (93%)
  local copies, waits for them, and re-layouts  5.33 us (7%)
    pallas_call x1, Pallas kernels, local(): pl.pallas_call(functools.partial(kernel, sizes), out_shape=jax.ShapeDtype...  74.4 us
    unnamed x10, local copies, waits for them, and re-layouts  4.63 us

profile of v1, /device:TPU:25, one launch (start us, length us, event | category | flops | bytes accessed | tf_op | source)
XLA Modules:
  0.0 79.8 jit_solution(11542366813428749219)
XLA Ops:
  0.0 0.0 copy-start.3
  0.0 0.7 broadcast_in_dim.6.place_ref
  0.7 0.0 copy-done.3
  0.7 0.8 %copy.9.named_ref = s32[2,64,16]{2,1,0:T(8,128)S(1)} copy(s32[2,64,16]{1,2,0:T(8,128)} %param.11) | data formatting | bytes 16384 | tf_op args[5]
  1.5 0.0 copy-start
  1.5 1.0 %copy-done = bf16[2,1,512,256]{3,2,1,0:T(8,128)(2,1)S(1)} copy-done((bf16[2,1,512,256]{3,2,1,0:T(8,128)(2,1)S(1)}, bf16[2,1,512,256]{3,2,1,0:T(8,128)(2,1)}, u32[]{:S(2)}) %copy-start) | copy-done | bytes 524312
  2.6 0.0 copy-start.1
  2.6 1.0 %copy-done.1 = bf16[2,1,512,256]{3,2,1,0:T(8,128)(2,1)S(1)} copy-done((bf16[2,1,512,256]{3,2,1,0:T(8,128)(2,1)S(1)}, bf16[2,1,512,256]{3,2,1,0:T(8,128)(2,1)}, u32[]{:S(2)}) %copy-start.1) | copy-done | bytes 524312
  3.6 0.0 copy-start.2
  3.6 0.9 %copy-done.2 = bf16[1,512,256]{2,1,0:T(8,128)(2,1)S(1)} copy-done((bf16[1,512,256]{2,1,0:T(8,128)(2,1)S(1)}, bf16[1,512,256]{2,1,0:T(8,128)(2,1)}, u32[]{:S(2)}) %copy-start.2) | copy-done | bytes 262168
  4.5 74.4 %shard_map.64 = f32[1,512,256]{2,1,0:T(8,128)S(1)} custom-call(bf16[1,512,256]{2,1,0:T(8,128)(2,1)S(1)} %copy-done.2, bf16[1,512]{1,0:T(2,128)(2,1)S(1)} %broadcast_in_dim.6.place_ref, bf16[2,1,512,256]{3,2,1,0:T(8,128)(2,1)S(1)} %copy-done, bf16[2,1,512]{2,1,0:T(2,128)(2,1)S(1)} %copy.8.obs_place_ref, bf16[2,1,512,256]{3,2,1,0:T(8,128)(2,1)S(1)} %copy-done.1, ...), custom_call_target="tpu_custom_call" | custom-call | flops 8589934592 | bytes 4194304 | tf_op jit(solution)/shard_map/pallas_call | solution.py:273
  79.0 0.8 copy.11
  (1 shorter events, 0.0 us)
Async XLA Ops:
  0.0 0.7 copy-start.3
  1.5 1.0 %copy-start = (bf16[2,1,512,256]{3,2,1,0:T(8,128)(2,1)S(1)}, bf16[2,1,512,256]{3,2,1,0:T(8,128)(2,1)}, u32[]{:S(2)}) copy-start(bf16[2,1,512,256]{3,2,1,0:T(8,128)(2,1)} %obs_ref.1) | copy-start | bytes 1572868
  2.6 1.0 %copy-start.1 = (bf16[2,1,512,256]{3,2,1,0:T(8,128)(2,1)S(1)}, bf16[2,1,512,256]{3,2,1,0:T(8,128)(2,1)}, u32[]{:S(2)}) copy-start(bf16[2,1,512,256]{3,2,1,0:T(8,128)(2,1)} %weight_ref.1) | copy-start | bytes 1572868
  3.6 0.9 %copy-start.2 = (bf16[1,512,256]{2,1,0:T(8,128)(2,1)S(1)}, bf16[1,512,256]{2,1,0:T(8,128)(2,1)}, u32[]{:S(2)}) copy-start(bf16[1,512,256]{2,1,0:T(8,128)(2,1)} %state_ref.1) | copy-start | bytes 786436

commit v2 on v1

--- a/solution.py
+++ b/solution.py
@@ -10,13 +10,15 @@
 
 LANES = 128
 UNIT = 256
+UNROLL = 4
 STRETCH = 2.0 * math.sqrt(math.log2(math.e))
 MASKED = -1e30
 
 
 def kernel(sizes, state_ref, place_ref, obs_ref, obs_place_ref, weight_ref, named_ref, out_ref,
            states, columns, obs, weights, places, place_send, obs_places, obs_place_send, masks, total, shares, arrived,
-           state_s, state_r, place_s, place_r, obs_s, obs_r, weight_s, weight_r, op_s, op_r, share_s, share_r, own_sem):
+           state_s, state_r, place_s, place_r, obs_s, obs_r, weight_s, weight_r, op_s, op_r, share_s, share_r, own_sem,
+           hop, hop_sem):
     n_rows, n_obs, own_rows, obs_rows, blocks, batches = sizes
     edge = obs_rows // blocks
     members = state_ref.shape[-1]
@@ -167,6 +169,25 @@
         else:
             own_weights[t].wait()
 
+    per_source = own_rows // UNIT
+    early = [(0, t) for t in range(batches)] if per_source else []
+
+    def sweep(chunk, first_unit, count):
+        def step(i, carry):
+            unit(*chunk, first_unit + i)
+            return carry
+        lax.fori_loop(0, count, step, 0, unroll=math.gcd(count, UNROLL))
+
+    def early_source(k):
+        state_arrival(k).wait_recv()
+        for u in range(per_source):
+            for chunk in early:
+                unit(*chunk, lax.rem(o - k + n_obs, n_obs) * per_source + u)
+
+    for chunk in early:
+        pieces_in(*chunk)
+    early_source(0)
+
     if forward:
         for t in range(batches):
             came = 1 if t % 2 == 0 else 2
@@ -177,20 +198,17 @@
     else:
         done = set()
 
-    for k in range(n_obs):
-        state_arrival(k).wait_recv()
-
-    chunks = [(0, t) for t in range(batches)] + sorted(done)
-    chunks += [(d, t) for d in range(1, n_rows) for t in range(batches) if (d, t) not in done]
+    for k in sorted(range(1, n_obs), key=lambda k: min(k, n_obs - k)):
+        early_source(k)
+    done.update(early)
+
+    chunks = sorted(done - set(early))
+    chunks += [(d, t) for d in range(n_rows) for t in range(batches) if (d, t) not in done]
     last = chunks[-batches:]
     for chunk in chunks[:-batches]:
         if chunk not in done:
             pieces_in(*chunk)
-
-        def sweep(index, carry, chunk=chunk):
-            unit(*chunk, index)
-            return carry
-        lax.fori_loop(0, span // UNIT, sweep, 0)
+        sweep(chunk, 0, span // UNIT)
 
     for chunk in last:
         if chunk not in done:
@@ -204,12 +222,44 @@
         return remote(shares.at[pl.ds(pl.multiple_of(d * own_rows, own_rows), own_rows)], arrived.at[o],
                       share_s.at[d], share_r.at[o], at(r, h, d))
 
+    relay = n_obs == 4 and group == own_rows
+    mirror = o // 2
+    inner = o + mirror * (3 - 2 * o)
+
+    def hop_copy(d):
+        return remote(shares.at[pl.ds(pl.multiple_of(d * own_rows, own_rows), own_rows)], hop, hop_sem.at[0],
+                      hop_sem.at[1], at(r, h, 1 + mirror))
+
     def finish(g, carry):
-        which = lax.rem(own_group + 1 + g, groups)
+        if relay:
+            towards = (1 - inner) * (3 - g) + inner * lax.rem(2 + 3 * g, 5)
+            which = towards + mirror * (3 - 2 * towards)
+        else:
+            which = lax.rem(own_group + 1 + g, groups)
         for u in range(group // UNIT):
             for chunk in last:
                 unit(*chunk, which * (group // UNIT) + u)
         start = pl.multiple_of(which * group, group)
+        if relay:
+            apart = (which - o) * (which - o)
+
+            @pl.when(apart == 9)
+            def _():
+                shares[pl.ds(start, group), :] = total[pl.ds(start, group), :].astype(jnp.bfloat16)
+                hop_copy(which).start()
+
+            @pl.when((apart == 4) & (inner == 1))
+            def _():
+                hop_copy(which).wait_recv()
+                shares[pl.ds(start, group), :] = (
+                    total[pl.ds(start, group), :] + hop[...].astype(jnp.float32)).astype(jnp.bfloat16)
+                share_copy(which).start()
+
+            @pl.when((apart == 1) | ((apart == 4) & (inner == 0)))
+            def _():
+                shares[pl.ds(start, group), :] = total[pl.ds(start, group), :].astype(jnp.bfloat16)
+                share_copy(which).start()
+            return carry
         shares[pl.ds(start, group), :] = total[pl.ds(start, group), :].astype(jnp.bfloat16)
         for j in range(group // own_rows):
             d = which * (group // own_rows) + j
@@ -226,14 +276,30 @@
 
     def collect(k, carry):
         source = other(k)
-        remote(shares.at[pl.ds(mine, own_rows)], arrived.at[source], share_s.at[source], share_r.at[source],
-               at(r, h, source)).wait_recv()
-        out_ref[0] += arrived[source].astype(jnp.float32)
+
+        def take():
+            remote(shares.at[pl.ds(mine, own_rows)], arrived.at[source], share_s.at[source], share_r.at[source],
+                   at(r, h, source)).wait_recv()
+            out_ref[0] += arrived[source].astype(jnp.float32)
+        if relay:
+            pl.when((source - o) * (source - o) != 9)(take)
+        else:
+            take()
         return carry
     lax.fori_loop(1, n_obs, collect, 0)
 
     def left(k, carry):
-        share_copy(other(k)).wait_send()
+        d = other(k)
+        if relay:
+            @pl.when((d - o) * (d - o) == 9)
+            def _():
+                hop_copy(d).wait_send()
+
+            @pl.when((d - o) * (d - o) != 9)
+            def _():
+                share_copy(d).wait_send()
+        else:
+            share_copy(d).wait_send()
         return carry
     lax.fori_loop(1, n_obs, left, 0)
     for k in range(n_obs):
@@ -269,7 +335,7 @@
     dma = pltpu.SemaphoreType.DMA
     f32, bf16 = jnp.float32, jnp.bfloat16
     whole = pl.BlockSpec(memory_space=pltpu.VMEM)
-    hbm = pl.BlockSpec(memory_space=pl.ANY)
+    hbm = pl.BlockSpec(memory_space=pltpu.HBM)
     return pl.pallas_call(
         functools.partial(kernel, sizes),
         out_shape=jax.ShapeDtypeStruct(ens_state.shape, f32),
@@ -291,8 +357,9 @@
             dma((n_obs,)), dma((n_obs,)), dma((n_obs,)), dma((n_obs,)),
             dma((n_rows, batches)), dma((n_rows, batches)), dma((n_rows, batches)), dma((n_rows, batches)),
             dma((n_rows,)), dma((n_rows,)), dma((n_obs,)), dma((n_obs,)), dma((batches,)),
+            pltpu.VMEM((own_rows, members), bf16), dma((2,)),
         ],
-        compiler_params=pltpu.CompilerParams(collective_id=0, has_side_effects=True, vmem_limit_bytes=48 * 2**20),
+        compiler_params=pltpu.CompilerParams(collective_id=0, has_side_effects=True, vmem_limit_bytes=40 * 2**20),
         cost_estimate=pl.CostEstimate(flops=4 * span * members * n_rows * batches * obs_rows,
                                       bytes_accessed=4 * 2**20,
                                       transcendentals=span * n_rows * batches * obs_rows),

time: 80.1 us -> 67.4 us (0.84)
  the two profiles are of different devices: /device:TPU:25 before, /device:TPU:0 now
where the time goes in v2:
time: 67.4 us; the launch traced here: 67.1 us
  Pallas kernels  61.8 us (92%)
  local copies, waits for them, and re-layouts  5.33 us (8%)
    pallas_call x1, Pallas kernels, local(): pl.pallas_call(functools.partial(kernel, sizes), out_shape=jax.ShapeDtype...  61.8 us
    unnamed x10, local copies, waits for them, and re-layouts  4.63 us

profile of v2, /device:TPU:0, one launch (start us, length us, event | category | flops | bytes accessed | tf_op | source)
XLA Modules:
  0.0 67.1 jit_solution(14912292559405415903)
XLA Ops:
  0.0 0.0 copy-start.3
  0.0 0.7 %broadcast_in_dim.6.place_ref = bf16[1,512]{1,0:T(2,128)(2,1)S(1)} reshape(bf16[512]{0:T(512)(128)(2,1)} %param.7) | data formatting | bytes 2048 | tf_op jit(solution)/shard_map/broadcast_in_dim | solution.py:331
  0.7 0.0 copy-done.3
  0.7 0.8 %copy.9.named_ref = s32[2,64,16]{2,1,0:T(8,128)S(1)} copy(s32[2,64,16]{1,2,0:T(8,128)} %param.11) | data formatting | bytes 16384 | tf_op args[5]
  1.5 0.0 copy-start
  1.5 1.0 %copy-done = bf16[2,1,512,256]{3,2,1,0:T(8,128)(2,1)S(1)} copy-done((bf16[2,1,512,256]{3,2,1,0:T(8,128)(2,1)S(1)}, bf16[2,1,512,256]{3,2,1,0:T(8,128)(2,1)}, u32[]{:S(2)}) %copy-start) | copy-done | bytes 524312
  2.6 0.0 copy-start.1
  2.6 1.0 %copy-done.1 = bf16[2,1,512,256]{3,2,1,0:T(8,128)(2,1)S(1)} copy-done((bf16[2,1,512,256]{3,2,1,0:T(8,128)(2,1)S(1)}, bf16[2,1,512,256]{3,2,1,0:T(8,128)(2,1)}, u32[]{:S(2)}) %copy-start.1) | copy-done | bytes 524312
  3.6 0.0 copy-start.2
  3.6 0.9 %copy-done.2 = bf16[1,512,256]{2,1,0:T(8,128)(2,1)S(1)} copy-done((bf16[1,512,256]{2,1,0:T(8,128)(2,1)S(1)}, bf16[1,512,256]{2,1,0:T(8,128)(2,1)}, u32[]{:S(2)}) %copy-start.2) | copy-done | bytes 262168
  4.5 61.8 %shard_map.64 = f32[1,512,256]{2,1,0:T(8,128)S(1)} custom-call(bf16[1,512,256]{2,1,0:T(8,128)(2,1)S(1)} %copy-done.2, bf16[1,512]{1,0:T(2,128)(2,1)S(1)} %broadcast_in_dim.6.place_ref, bf16[2,1,512,256]{3,2,1,0:T(8,128)(2,1)S(1)} %copy-done, bf16[2,1,512]{2,1,0:T(2,128)(2,1)S(1)} %copy.8.obs_place_ref, bf16[2,1,512,256]{3,2,1,0:T(8,128)(2,1)S(1)} %copy-done.1, ...), custom_call_target="tpu_custom_call" | custom-call | flops 8589934592 | bytes 4194304 | tf_op jit(solution)/shard_map/pallas_call | solution.py:339
  66.3 0.8 %copy.11 = f32[1,512,256]{2,1,0:T(8,128)} copy(f32[1,512,256]{2,1,0:T(8,128)S(1)} %shard_map.64) | data formatting | bytes 1048576
  (1 shorter events, 0.0 us)
Async XLA Ops:
  0.0 0.7 %copy-start.3 = (bf16[2,512]{1,0:T(2,128)(2,1)S(1)}, bf16[2,512]{1,0:T(2,128)(2,1)}, u32[]{:S(2)}) copy-start(bf16[2,512]{1,0:T(2,128)(2,1)} %param.9) | copy-start | bytes 6148
  1.5 1.0 %copy-start = (bf16[2,1,512,256]{3,2,1,0:T(8,128)(2,1)S(1)}, bf16[2,1,512,256]{3,2,1,0:T(8,128)(2,1)}, u32[]{:S(2)}) copy-start(bf16[2,1,512,256]{3,2,1,0:T(8,128)(2,1)} %obs_ref.1) | copy-start | bytes 1572868
  2.6 1.0 %copy-start.1 = (bf16[2,1,512,256]{3,2,1,0:T(8,128)(2,1)S(1)}, bf16[2,1,512,256]{3,2,1,0:T(8,128)(2,1)}, u32[]{:S(2)}) copy-start(bf16[2,1,512,256]{3,2,1,0:T(8,128)(2,1)} %weight_ref.1) | copy-start | bytes 1572868
  3.6 0.9 %copy-start.2 = (bf16[1,512,256]{2,1,0:T(8,128)(2,1)S(1)}, bf16[1,512,256]{2,1,0:T(8,128)(2,1)}, u32[]{:S(2)}) copy-start(bf16[1,512,256]{2,1,0:T(8,128)(2,1)} %state_ref.1) | copy-start | bytes 786436

commit v3 on v2

--- a/solution.py
+++ b/solution.py
@@ -116,13 +116,14 @@
 
     kept = -math.log2(members - 1)
     first = r * span_blocks
-    ids = lax.broadcasted_iota(jnp.int32, (span_blocks, 1), 0) + first
+    lanes = lax.broadcasted_iota(jnp.int32, (1, named_ref.shape[-1]), 1)
+    lists = [jnp.concatenate([jnp.max(jnp.where(named_ref[t] == first + i, 1.0, 0.0), axis=0, keepdims=True)
+                              for i in range(span_blocks)], axis=0) for t in range(batches)]
     for delta in range(n_rows):
         base = ((r ^ delta) * n_obs + o) * blocks
         for t in range(batches):
             def fill(b, carry, base=base, delta=delta, t=t):
-                named = named_ref[t, pl.ds(base + b, 1), :]
-                listed = jnp.max(jnp.where(named == ids, 1.0, 0.0), axis=1, keepdims=True)
+                listed = jnp.max(jnp.where(lanes == base + b, lists[t], 0.0), axis=1, keepdims=True)
                 masks[delta, t, b] = jnp.broadcast_to(jnp.where(listed > 0.5, kept, MASKED), (span_blocks, edge))
                 return carry
             lax.fori_loop(0, blocks, fill, 0)
@@ -363,7 +364,7 @@
         cost_estimate=pl.CostEstimate(flops=4 * span * members * n_rows * batches * obs_rows,
                                       bytes_accessed=4 * 2**20,
                                       transcendentals=span * n_rows * batches * obs_rows),
-    )(ens_state, place_row, obs_ens, obs_pos[:, None, :], innov_weight, block_rows)
+    )(ens_state, place_row, obs_ens, obs_pos[:, None, :], innov_weight, jnp.swapaxes(block_rows, 1, 2))
 
 
 def solution(mesh):

time: 67.4 us -> 67.4 us (level)
    broadcast_in_dim x1, local copies, waits for them, and re-layouts: 0.7 us -> 0.01 us  [local(): place_row = state_pos[None, :]]
    unnamed x10 -> x13, local copies, waits for them, and re-layouts: 4.63 us -> 5.23 us
where the time goes in v3:
time: 67.4 us; the launch traced here: 67 us
  Pallas kernels  61.8 us (92%)
  local copies, waits for them, and re-layouts  5.24 us (8%)
    pallas_call x1, Pallas kernels, local(): pl.pallas_call(functools.partial(kernel, sizes), out_shape=jax.ShapeDtype...  61.8 us
    unnamed x13, local copies, waits for them, and re-layouts  5.23 us

profile of v3, /device:TPU:0, one launch (start us, length us, event | category | flops | bytes accessed | tf_op | source)
XLA Modules:
  0.0 67.0 jit_solution(7976549590627089496)
XLA Ops:
  0.0 0.0 copy-start.5
  0.0 0.0 copy-start.4
  0.0 0.7 %copy-done.5 = bf16[512]{0:T(512)(128)(2,1)S(1)} copy-done((bf16[512]{0:T(512)(128)(2,1)S(1)}, bf16[512]{0:T(512)(128)(2,1)}, u32[]{:S(2)}) %copy-start.5) | copy-done | bytes 1048
  0.7 0.0 copy-done.4
  0.7 0.0 copy-start
  0.7 1.0 %copy-done = bf16[2,1,512,256]{3,2,1,0:T(8,128)(2,1)S(1)} copy-done((bf16[2,1,512,256]{3,2,1,0:T(8,128)(2,1)S(1)}, bf16[2,1,512,256]{3,2,1,0:T(8,128)(2,1)}, u32[]{:S(2)}) %copy-start) | copy-done | bytes 524312
  1.7 0.0 copy-start.1
  1.7 1.0 %copy-done.1 = bf16[2,1,512,256]{3,2,1,0:T(8,128)(2,1)S(1)} copy-done((bf16[2,1,512,256]{3,2,1,0:T(8,128)(2,1)S(1)}, bf16[2,1,512,256]{3,2,1,0:T(8,128)(2,1)}, u32[]{:S(2)}) %copy-start.1) | copy-done | bytes 524312
  2.8 0.0 copy-start.2
  2.8 0.9 %copy-done.2 = bf16[1,512,256]{2,1,0:T(8,128)(2,1)S(1)} copy-done((bf16[1,512,256]{2,1,0:T(8,128)(2,1)S(1)}, bf16[1,512,256]{2,1,0:T(8,128)(2,1)}, u32[]{:S(2)}) %copy-start.2) | copy-done | bytes 262168
  3.7 0.0 copy-start.3
  3.7 0.7 %copy-done.3 = s32[2,64,16]{1,2,0:T(8,128)S(1)} copy-done((s32[2,64,16]{1,2,0:T(8,128)S(1)}, s32[2,64,16]{1,2,0:T(8,128)}, u32[]{:S(2)}) %copy-start.3) | copy-done | bytes 8216
  4.5 61.8 %shard_map.64 = f32[1,512,256]{2,1,0:T(8,128)S(1)} custom-call(bf16[1,512,256]{2,1,0:T(8,128)(2,1)S(1)} %copy-done.2, bf16[1,512]{1,0:T(2,128)(2,1)S(1)} %broadcast_in_dim.6.place_ref, bf16[2,1,512,256]{3,2,1,0:T(8,128)(2,1)S(1)} %copy-done, bf16[2,1,512]{2,1,0:T(2,128)(2,1)S(1)} %copy.7.obs_place_ref, bf16[2,1,512,256]{3,2,1,0:T(8,128)(2,1)S(1)} %copy-done.1, ...), custom_call_target="tpu_custom_call" | custom-call | flops 8589934592 | bytes 4194304 | tf_op jit(solution)/shard_map/pallas_call | solution.py:340
  66.2 0.8 %copy.9 = f32[1,512,256]{2,1,0:T(8,128)} copy(f32[1,512,256]{2,1,0:T(8,128)S(1)} %shard_map.64) | data formatting | bytes 1048576
  (2 shorter events, 0.0 us)
Async XLA Ops:
  0.0 0.7 %copy-start.5 = (bf16[512]{0:T(512)(128)(2,1)S(1)}, bf16[512]{0:T(512)(128)(2,1)}, u32[]{:S(2)}) copy-start(bf16[512]{0:T(512)(128)(2,1)} %param.7) | copy-start | bytes 3076
  0.0 0.7 %copy-start.4 = (bf16[2,512]{1,0:T(2,128)(2,1)S(1)}, bf16[2,512]{1,0:T(2,128)(2,1)}, u32[]{:S(2)}) copy-start(bf16[2,512]{1,0:T(2,128)(2,1)} %param.9) | copy-start | bytes 6148
  0.7 1.0 %copy-start = (bf16[2,1,512,256]{3,2,1,0:T(8,128)(2,1)S(1)}, bf16[2,1,512,256]{3,2,1,0:T(8,128)(2,1)}, u32[]{:S(2)}) copy-start(bf16[2,1,512,256]{3,2,1,0:T(8,128)(2,1)} %obs_ref.1) | copy-start | bytes 1572868
  1.7 1.0 %copy-start.1 = (bf16[2,1,512,256]{3,2,1,0:T(8,128)(2,1)S(1)}, bf16[2,1,512,256]{3,2,1,0:T(8,128)(2,1)}, u32[]{:S(2)}) copy-start(bf16[2,1,512,256]{3,2,1,0:T(8,128)(2,1)} %weight_ref.1) | copy-start | bytes 1572868
  2.8 0.9 %copy-start.2 = (bf16[1,512,256]{2,1,0:T(8,128)(2,1)S(1)}, bf16[1,512,256]{2,1,0:T(8,128)(2,1)}, u32[]{:S(2)}) copy-start(bf16[1,512,256]{2,1,0:T(8,128)(2,1)} %state_ref.1) | copy-start | bytes 786436
  3.7 0.7 %copy-start.3 = (s32[2,64,16]{1,2,0:T(8,128)S(1)}, s32[2,64,16]{1,2,0:T(8,128)}, u32[]{:S(2)}) copy-start(s32[2,64,16]{1,2,0:T(8,128)} %param.11) | copy-start | bytes 24580
